TPU v7x, 128 devices: a whole 4x4x4 slice. The times are simulated.
128 devices in a mesh: comp: 4 (over z_hi, core), tile: 32 (over x, y, z_lo).
Axes of the slice: x: 4, y: 4, z: 4 (z_hi: 2, z_lo: 2; z = z_hi * 2 + z_lo), core: 2. Of those that a mesh axis runs over, the one named last changes fastest.
Arguments:
- state: float32 [4, 4, 31, 12288], P('comp', None, None, 'tile'), may hold values from -6 to 6
- velocity: float32 [4, 2, 31, 12288], P('comp', None, None, 'tile'), may hold values from -4 to 4
- wet_mask: int32 [31, 12288], P(None, 'tile'), may hold values 0 or 1
- margin_source: int32 [4, 32, 279], P('comp', 'tile'), may hold values from 0 to 92
- margin_dest: int32 [4, 32, 279], P('comp', 'tile'), may hold values from 0 to 127, as said below
- margin_block: int32 [4, 32, 279], P('comp', 'tile'), may hold values from 0 to 92
- margin_weight: bfloat16 [4, 32, 279, 128, 128], P('comp', 'tile'), may hold values from -0.375 to 0.375
Outputs:
- new_state: float32 [4, 4, 31, 12288], P('comp', None, None, 'tile')
- coupled_fields: float32 [4, 2, 31, 12288], P('comp', None, None, 'tile')
Inputs may be any that keep to these rules, and one draw needn't show every extreme that they name: `margin_dest`: the device numbered c * 32 + t. Rows held by atmosphere devices name ocean devices; rows held by ocean devices name atmosphere devices. A row held by a device of tile index t names a tile index within two of t, counted periodically over the 32 indices. Of one device's 279 rows at most 111 name devices of one tile index, and on every device some tile index is named exactly 111 times.
All inputs are finite; a program needn't handle non-finite values. No bound on the sum of `wet_mask` on one device may be relied on, other than what follows from the above.
Results may differ from a plain program's by a relative error of at most 0.0029.
Values sent between devices are 32-bit elements; how exact they have to be, the bound alone decides.
A program may use at most 64 MiB of HBM per device.

v0:
```python
import functools

import jax
import jax.numpy as jnp
import numpy as np
from jax import lax
from jax.experimental import pallas as pl
from jax.experimental.pallas import tpu as pltpu
from jax.sharding import PartitionSpec as P

MESH = pl.DeviceIdType.MESH

atmos_step = 0.02
viscosity = 0.3
ocean_step = 0.1
diffusivity = 0.2
vertical_mix = 0.5
heat_coef = 0.5
salt_coef = 0.5

LANES = 128
GROUP = 8
CHUNK = 40
OFFSETS = (0, 4, 1, 3, 2)


def gll_tables():
    nodes = np.array([-1.0, -1.0 / np.sqrt(5.0), 1.0 / np.sqrt(5.0), 1.0])
    weights = np.array([1.0 / 6.0, 5.0 / 6.0, 5.0 / 6.0, 1.0 / 6.0])
    legendre = (5.0 * nodes**3 - 3.0 * nodes) / 2.0
    deriv = np.zeros((4, 4))
    for row_node in range(4):
        for col_node in range(4):
            if row_node != col_node:
                deriv[row_node, col_node] = legendre[row_node] / (
                    legendre[col_node] * (nodes[row_node] - nodes[col_node])
                )
    deriv[0, 0] = -3.0
    deriv[3, 3] = 3.0
    return deriv, weights


def stencils():
    deriv, weights = gll_tables()
    stiff = np.einsum("k,kj,km->jm", weights, deriv, deriv)
    derivative = np.zeros((5, 7))
    stiffness = np.zeros((5, 7))
    for kind, holders in enumerate(((0, 3), (1,), (2,), (0,), (3,))):
        total = sum(weights[j] for j in holders)
        for j in holders:
            for m in range(4):
                derivative[kind, m - j + 3] += weights[j] * deriv[j, m] / total
                stiffness[kind, m - j + 3] += stiff[j, m] / total
    return derivative, stiffness


def by_kind(kinds, values):
    out = jnp.full(kinds.shape, float(values[0]), jnp.float32)
    for kind in range(1, len(values)):
        out = jnp.where(kinds == kind, float(values[kind]), out)
    return out


def kernel(
    sizes,
    state_hbm,
    velocity_hbm,
    wet_hbm,
    source_hbm,
    dest_hbm,
    block_hbm,
    weight_hbm,
    new_ref,
    coupled_ref,
    state,
    velocity,
    wet,
    source,
    dest,
    block,
    weight,
    payload,
    picked,
    pieces,
    fields,
    strips,
    edges,
    outbox,
    inbox,
    load_sem,
    chunk_sem,
    out_sem,
    in_sem,
    strip_sem,
    edge_sem,
):
    comps, tiles, rows, width, margins = sizes
    ocean = comps - 1
    padded = rows + 1
    parts = width // LANES
    span = parts * padded
    wide = width + LANES
    me = lax.axis_index("comp")
    tile = lax.axis_index("tile")

    def tile_at(step):
        return lax.rem(tile + step + tiles, tiles)

    def device(comp, step):
        return {"comp": comp, "tile": tile_at(step)}

    barrier = pltpu.get_barrier_semaphore()

    def greet(comp, step):
        pl.semaphore_signal(
            barrier, inc=1, device_id=device(comp, step), device_id_type=MESH
        )

    greet(me, -1)
    greet(me, 1)

    @pl.when(me == ocean)
    def _():
        for k in range(5):
            for comp in range(ocean):
                greet(comp, k - 2)

    @pl.when(me != ocean)
    def _():
        for k in range(5):
            greet(ocean, k - 2)

    loads = [
        pltpu.make_async_copy(src, dst, load_sem.at[i])
        for i, (src, dst) in enumerate(
            (
                (source_hbm, source),
                (state_hbm, state),
                (dest_hbm, dest),
                (block_hbm, block),
                (velocity_hbm, velocity),
                (wet_hbm, wet),
            )
        )
    ]
    bounds = [(low, min(low + CHUNK, margins)) for low in range(0, margins, CHUNK)]
    chunks = [
        pltpu.make_async_copy(
            weight_hbm.at[0, 0, pl.ds(low, high - low)],
            weight.at[pl.ds(low, high - low)],
            chunk_sem.at[i],
        )
        for i, (low, high) in enumerate(bounds)
    ]
    for copy in loads[:4] + chunks + loads[4:]:
        copy.start()

    payload[...] = jnp.zeros_like(payload)
    pieces[pl.ds(margins // 8 * 8, pieces.shape[0] - margins // 8 * 8), :] = jnp.zeros(
        (pieces.shape[0] - margins // 8 * 8, 2 * LANES), jnp.float32
    )
    loads[0].wait()
    loads[1].wait()
    for a in range(2):
        for part in range(parts):
            payload[pl.ds(part * padded, rows), pl.ds(a * LANES, LANES)] = state[
                0, 2 * a, :, pl.ds(part * LANES, LANES)
            ]

    def place_of(numbers):
        row = (numbers * 171) >> 9
        return (numbers - 3 * row) * padded + row

    slots = lax.broadcasted_iota(jnp.int32, (span, margins), 0)
    chosen = (slots == place_of(source[0])).astype(jnp.float32)
    picked[pl.ds(0, margins), :] = lax.dot_general(
        chosen.T.astype(jnp.bfloat16),
        payload[...].astype(jnp.bfloat16),
        (((1,), (0,)), ((), ())),
        preferred_element_type=jnp.float32,
    )

    for s in range(4):
        fields[s, pl.ds(0, rows), pl.ds(0, width)] = state[0, s]
    loads[4].wait()
    loads[5].wait()
    fields[4, pl.ds(0, rows), pl.ds(0, width)] = velocity[0, 0]
    fields[5, pl.ds(0, rows), pl.ds(0, width)] = wet[...].astype(jnp.float32)
    fields[6, pl.ds(0, rows), pl.ds(0, width)] = velocity[0, 1]
    for s in range(7):
        fields[s, pl.ds(rows, 1), pl.ds(0, width)] = jnp.zeros((1, width), jnp.float32)
    lane = lax.broadcasted_iota(jnp.int32, (padded, LANES), 1)
    right_going = fields[0, :, pl.ds(width - LANES, LANES)]
    left_going = fields[0, :, pl.ds(0, LANES)]
    for s in range(1, 6):
        moved = pltpu.roll(fields[s, :, pl.ds(width - LANES, LANES)], LANES - 4 * s, 1)
        right_going = jnp.where(lane < LANES - 4 * s, moved, right_going)
        moved = pltpu.roll(fields[s, :, pl.ds(0, LANES)], 4 * s, 1)
        left_going = jnp.where(lane >= 4 * s, moved, left_going)
    strips[0] = right_going
    strips[1] = left_going

    rank = lax.rem(lax.broadcasted_iota(jnp.int32, (2 * GROUP, LANES), 0), GROUP)
    for (low, high), copy in zip(bounds, chunks):
        copy.wait()
        for first in range(low, high, GROUP):
            count = min(GROUP, high - first)
            held = jnp.concatenate(
                [picked[pl.ds(first, GROUP), pl.ds(a * LANES, LANES)] for a in range(2)], 0
            )
            spread = jnp.concatenate(
                [jnp.where(rank == i, held, 0.0).astype(jnp.bfloat16) for i in range(count)], 1
            )
            product = jnp.dot(
                spread,
                weight[pl.ds(first, count)].reshape(count * LANES, LANES),
                preferred_element_type=jnp.float32,
            )
            for a in range(2):
                pieces[pl.ds(first, count), pl.ds(a * LANES, LANES)] = product[
                    a * GROUP : a * GROUP + count
                ]

    loads[2].wait()
    loads[3].wait()
    target = dest[0]
    offset = (target & (tiles - 1)) - tile + 2
    offset = jnp.where(offset < 0, offset + tiles, offset)
    offset = jnp.where(offset >= tiles, offset - tiles, offset)
    place = place_of(block[0])
    whole = pieces[...]
    coarse = whole.astype(jnp.bfloat16)
    fine = (whole - coarse.astype(jnp.float32)).astype(jnp.bfloat16)

    def gathered(codes, low, count):
        numbers = lax.broadcasted_iota(jnp.int32, (count, margins), 0) + low
        onehot = (numbers == codes).astype(jnp.float32).astype(jnp.bfloat16)
        return jnp.dot(
            onehot, coarse[:margins], preferred_element_type=jnp.float32
        ) + jnp.dot(onehot, fine[:margins], preferred_element_type=jnp.float32)

    def message(slot, far_slot, comp, k):
        return pltpu.make_async_remote_copy(
            src_ref=outbox.at[slot],
            dst_ref=inbox.at[far_slot],
            send_sem=out_sem.at[slot],
            recv_sem=in_sem.at[far_slot],
            device_id=device(comp, k - 2),
            device_id_type=MESH,
        )

    def strip(side):
        return pltpu.make_async_remote_copy(
            src_ref=strips.at[side],
            dst_ref=edges.at[side],
            send_sem=strip_sem.at[side],
            recv_sem=edge_sem.at[side],
            device_id=device(me, 1 - 2 * side),
            device_id_type=MESH,
        )

    @pl.when(me == ocean)
    def _():
        pl.semaphore_wait(barrier, 2 + 5 * ocean)
        codes = (offset * ocean + (target >> 5)) * span + place
        for k in OFFSETS:
            out = gathered(codes, k * ocean * span, ocean * span)
            for comp in range(ocean):
                outbox[comp * 5 + k] = out[comp * span : (comp + 1) * span]
                message(comp * 5 + k, k, comp, k).start()

    @pl.when(me != ocean)
    def _():
        pl.semaphore_wait(barrier, 2 + 5)
        codes = offset * span + place
        for k in OFFSETS:
            outbox[k] = gathered(codes, k * span, span)
            message(k, me * 5 + k, ocean, k).start()

    for side in range(2):
        strip(side).start()
    for side in range(2):
        strip(side).wait()

    for s in range(6):
        after = pltpu.roll(edges[1], (LANES - 4 * s) % LANES, 1)
        before = pltpu.roll(edges[0], 4 * s, 1)
        fields[s, :, pl.ds(width, LANES)] = jnp.where(
            lane == 0, after, jnp.where(lane >= LANES - 3, before, 0.0)
        )

    def total(count):
        out = None
        for slot in range(count):
            pltpu.make_async_copy(inbox.at[slot], inbox.at[slot], in_sem.at[slot]).wait()
            out = inbox[slot] if out is None else out + inbox[slot]
        return out

    def give(out):
        for a in range(2):
            for part in range(parts):
                coupled_ref[0, a, :, pl.ds(part * LANES, LANES)] = out[
                    part * padded : part * padded + rows, a * LANES : (a + 1) * LANES
                ]

    def sent(count):
        for slot in range(count):
            pltpu.make_async_copy(
                outbox.at[slot], outbox.at[slot], out_sem.at[slot]
            ).wait()

    @pl.when(me != ocean)
    def _():
        derivative, stiffness = stencils()
        columns = lax.rem(lax.broadcasted_iota(jnp.int32, (padded, width), 1), 3)
        row = lax.broadcasted_iota(jnp.int32, (padded, width), 0)
        row_kind = lax.rem(row, 3)
        row_kind = jnp.where(row == 0, 3, jnp.where(row == rows - 1, 4, row_kind))
        east = fields[4, :, pl.ds(0, width)]
        north = fields[6, :, pl.ds(0, width)]
        for s in range(4):
            along_x = along_y = stiff = None
            whole = fields[s]
            centre = fields[s, :, pl.ds(0, width)]
            for k in range(7):
                step = k - 3
                shifted = whole if step == 0 else pltpu.roll(whole, (-step) % wide, 1)
                shifted = shifted[:, :width]
                first = by_kind(columns, derivative[:3, k]) * shifted
                second = by_kind(columns, stiffness[:3, k]) * shifted
                shifted = centre if step == 0 else pltpu.roll(centre, (-step) % padded, 0)
                third = by_kind(row_kind, derivative[:, k]) * shifted
                second += by_kind(row_kind, stiffness[:, k]) * shifted
                along_x = first if k == 0 else along_x + first
                along_y = third if k == 0 else along_y + third
                stiff = second if k == 0 else stiff + second
            out = centre - atmos_step * (
                2.0 * (east * along_x + north * along_y) + 4.0 * viscosity * stiff
            )
            new_ref[0, s] = out[:rows]
        give(total(5))
        sent(5)

    @pl.when(me == ocean)
    def _():
        p = fields[4]
        m = fields[5]
        m_centre = m[:, :width]
        q = fields[6, :, pl.ds(0, width)]
        m_x = m * pltpu.roll(m, wide - 1, 1)
        p_x = 0.25 * (p + pltpu.roll(p, wide - 1, 1))
        m_y = m_centre * pltpu.roll(m_centre, padded - 1, 0)
        q_y = 0.25 * (q + pltpu.roll(q, padded - 1, 0))
        base = []
        for s in range(4):
            u = fields[s]
            u_next = pltpu.roll(u, wide - 1, 1)
            flux = m_x * (p_x * (u + u_next) - diffusivity * (u_next - u))
            change = (flux - pltpu.roll(flux, 1, 1))[:, :width]
            u = u[:, :width]
            u_next = pltpu.roll(u, padded - 1, 0)
            flux = m_y * (q_y * (u + u_next) - diffusivity * (u_next - u))
            change = change + (flux - pltpu.roll(flux, 1, 0))
            other = fields[s ^ 1, :, pl.ds(0, width)]
            step = vertical_mix * (other - u) - change
            fields[s, :, pl.ds(0, width)] = u
            base.append(step)
        for s in (1, 3):
            u = fields[s, :, pl.ds(0, width)]
            new_ref[0, s] = (u + m_centre * (ocean_step * base[s]))[:rows]
        out = total(5 * ocean)
        give(out)
        for a, coef in ((0, heat_coef), (1, salt_coef)):
            s = 2 * a
            u = fields[s, :, pl.ds(0, width)]
            surface = jnp.concatenate(
                [
                    out[part * padded : (part + 1) * padded, a * LANES : (a + 1) * LANES]
                    for part in range(parts)
                ],
                1,
            )
            step = base[s] + coef * (surface - u)
            new_ref[0, s] = (u + m_centre * (ocean_step * step))[:rows]
        sent(5 * ocean)


def local(sizes, *arrays):
    comps, tiles, rows, width, margins = sizes
    parts = width // LANES
    padded = rows + 1
    span = parts * padded
    chunks = -(-margins // CHUNK)
    roomy = -(-margins // LANES) * LANES
    state, velocity, wet = arrays[:3]
    slots = 5 * (comps - 1)
    return pl.pallas_call(
        functools.partial(kernel, sizes),
        out_shape=(
            jax.ShapeDtypeStruct(state.shape, jnp.float32),
            jax.ShapeDtypeStruct(velocity.shape, jnp.float32),
        ),
        in_specs=[pl.BlockSpec(memory_space=pl.ANY)] * len(arrays),
        out_specs=(pl.BlockSpec(memory_space=pltpu.VMEM),) * 2,
        scratch_shapes=[
            *[pltpu.VMEM(array.shape, array.dtype) for array in arrays[:6]],
            pltpu.VMEM(arrays[6].shape[2:], jnp.bfloat16),
            pltpu.VMEM((span, 2 * LANES), jnp.float32),
            pltpu.VMEM((roomy, 2 * LANES), jnp.float32),
            pltpu.VMEM((roomy, 2 * LANES), jnp.float32),
            pltpu.VMEM((7, padded, width + LANES), jnp.float32),
            pltpu.VMEM((2, padded, LANES), jnp.float32),
            pltpu.VMEM((2, padded, LANES), jnp.float32),
            pltpu.VMEM((slots, span, 2 * LANES), jnp.float32),
            pltpu.VMEM((slots, span, 2 * LANES), jnp.float32),
            pltpu.SemaphoreType.DMA((6,)),
            pltpu.SemaphoreType.DMA((chunks,)),
            pltpu.SemaphoreType.DMA((slots,)),
            pltpu.SemaphoreType.DMA((slots,)),
            pltpu.SemaphoreType.DMA((2,)),
            pltpu.SemaphoreType.DMA((2,)),
        ],
        compiler_params=pltpu.CompilerParams(
            collective_id=0, has_side_effects=True, vmem_limit_bytes=56 * 2**20
        ),
    )(*arrays)


def solution(mesh):
    comps, tiles = mesh.shape["comp"], mesh.shape["tile"]

    def whole(*arrays):
        rows, width = arrays[0].shape[2:]
        sizes = (comps, tiles, rows, width // tiles, arrays[3].shape[-1])
        placed = (
            P("comp", None, None, "tile"),
            P("comp", None, None, "tile"),
            P(None, "tile"),
            P("comp", "tile", None),
            P("comp", "tile", None),
            P("comp", "tile", None),
            P("comp", "tile", None, None, None),
        )
        return jax.shard_map(
            functools.partial(local, sizes),
            mesh=mesh,
            in_specs=placed,
            out_specs=(P("comp", None, None, "tile"), P("comp", None, None, "tile")),
            check_vma=False,
        )(*arrays)

    return whole
```

profile of v0, /device:TPU:1, one launch (start us, length us, event | category | flops | bytes accessed | tf_op | source)
XLA Modules:
  0.0 33.6 jit_solution(8735707228345999742)
XLA Ops:
  0.6 1.5 %copy.10.velocity_hbm = f32[1,2,31,384]{3,2,1,0:T(8,128)} copy(f32[1,2,31,384]{3,1,2,0:T(2,128)} %param.8) | data formatting | bytes 190464 | tf_op args[1]
  2.2 1.6 %copy.9.state_hbm = f32[1,4,31,384]{3,2,1,0:T(8,128)} copy(f32[1,4,31,384]{3,1,2,0:T(4,128)} %param.7) | data formatting | bytes 380928 | tf_op args[0]
  3.8 26.5 %shard_map.86 = (f32[1,4,31,384]{3,2,1,0:T(8,128)}, f32[1,2,31,384]{3,2,1,0:T(8,128)}) custom-call(f32[1,4,31,384]{3,2,1,0:T(8,128)} %copy.9.state_hbm, f32[1,2,31,384]{3,2,1,0:T(8,128)} %copy.10.velocity_hbm, s32[31,384]{1,0:T(8,128)} %wet_hbm.1, s32[1,1,279]{2,1,0:T(1,128)} %source_hbm.1, s32[1,1,279]{2,1,0:T(1,128)} %dest_hbm.1, s32[1,1,279]{2,1,0:T(1,128)} %block_hbm.1, ...), custom_call_target="tpu_custom_call" | custom-call | tf_op jit(solution)/shard_map/pallas_call | solution.py:397
  30.3 1.7 %copy.11 = f32[1,4,31,384]{3,1,2,0:T(4,128)} copy(f32[1,4,31,384]{3,2,1,0:T(8,128)} %get-tuple-element.2) | data formatting | bytes 380928 | tf_op jit(solution)/shard_map/pallas_call | solution.py:397
  32.0 1.6 %copy.12 = f32[1,2,31,384]{3,1,2,0:T(2,128)} copy(f32[1,2,31,384]{3,2,1,0:T(8,128)} %get-tuple-element.3) | data formatting | bytes 190464 | tf_op jit(solution)/shard_map/pallas_call | solution.py:397
where the time goes:
time: 33.8 us; the launch traced here: 33.6 us
  Pallas kernels  26.5 us (78%)
  local copies, waits for them, and re-layouts  6.48 us (19%)
  between operations  0.64 us (2%)
    pallas_call x1, Pallas kernels, local(): pl.pallas_call(functools.partial(kernel, sizes), out_shape=(jax.ShapeDtyp...  26.5 us
    pallas_call x2, local copies, waits for them, and re-layouts, local(): pl.pallas_call(functools.partial(kernel, sizes), out_shape=(jax.ShapeDtyp...  3.33 us
    unnamed x2, local copies, waits for them, and re-layouts  3.15 us

commit v1 on v0

--- a/solution.py
+++ b/solution.py
@@ -70,8 +70,8 @@
     dest_hbm,
     block_hbm,
     weight_hbm,
-    new_ref,
-    coupled_ref,
+    new_hbm,
+    coupled_hbm,
     state,
     velocity,
     wet,
@@ -135,10 +135,14 @@
         for i, (src, dst) in enumerate(
             (
                 (source_hbm, source),
-                (state_hbm, state),
+                (state_hbm.at[0, :, 0, :], state.at[0]),
+                (state_hbm.at[0, :, 2, :], state.at[2]),
                 (dest_hbm, dest),
                 (block_hbm, block),
-                (velocity_hbm, velocity),
+                (state_hbm.at[0, :, 1, :], state.at[1]),
+                (state_hbm.at[0, :, 3, :], state.at[3]),
+                (velocity_hbm.at[0, :, 0, :], velocity.at[0]),
+                (velocity_hbm.at[0, :, 1, :], velocity.at[1]),
                 (wet_hbm, wet),
             )
         )
@@ -152,19 +156,19 @@
         )
         for i, (low, high) in enumerate(bounds)
     ]
-    for copy in loads[:4] + chunks + loads[4:]:
+    for copy in loads[:5] + chunks + loads[5:]:
         copy.start()
 
     payload[...] = jnp.zeros_like(payload)
     pieces[pl.ds(margins // 8 * 8, pieces.shape[0] - margins // 8 * 8), :] = jnp.zeros(
         (pieces.shape[0] - margins // 8 * 8, 2 * LANES), jnp.float32
     )
-    loads[0].wait()
-    loads[1].wait()
+    for copy in loads[:3]:
+        copy.wait()
     for a in range(2):
         for part in range(parts):
             payload[pl.ds(part * padded, rows), pl.ds(a * LANES, LANES)] = state[
-                0, 2 * a, :, pl.ds(part * LANES, LANES)
+                2 * a, :, pl.ds(part * LANES, LANES)
             ]
 
     def place_of(numbers):
@@ -180,13 +184,13 @@
         preferred_element_type=jnp.float32,
     )
 
+    for copy in loads[5:]:
+        copy.wait()
     for s in range(4):
-        fields[s, pl.ds(0, rows), pl.ds(0, width)] = state[0, s]
-    loads[4].wait()
-    loads[5].wait()
-    fields[4, pl.ds(0, rows), pl.ds(0, width)] = velocity[0, 0]
+        fields[s, pl.ds(0, rows), pl.ds(0, width)] = state[s]
+    fields[4, pl.ds(0, rows), pl.ds(0, width)] = velocity[0]
     fields[5, pl.ds(0, rows), pl.ds(0, width)] = wet[...].astype(jnp.float32)
-    fields[6, pl.ds(0, rows), pl.ds(0, width)] = velocity[0, 1]
+    fields[6, pl.ds(0, rows), pl.ds(0, width)] = velocity[1]
     for s in range(7):
         fields[s, pl.ds(rows, 1), pl.ds(0, width)] = jnp.zeros((1, width), jnp.float32)
     lane = lax.broadcasted_iota(jnp.int32, (padded, LANES), 1)
@@ -221,8 +225,8 @@
                     a * GROUP : a * GROUP + count
                 ]
 
-    loads[2].wait()
     loads[3].wait()
+    loads[4].wait()
     target = dest[0]
     offset = (target & (tiles - 1)) - tile + 2
     offset = jnp.where(offset < 0, offset + tiles, offset)
@@ -296,12 +300,21 @@
             out = inbox[slot] if out is None else out + inbox[slot]
         return out
 
+    stores = [
+        pltpu.make_async_copy(state.at[s], new_hbm.at[0, :, s, :], load_sem.at[s])
+        for s in range(4)
+    ] + [
+        pltpu.make_async_copy(velocity.at[a], coupled_hbm.at[0, :, a, :], load_sem.at[4 + a])
+        for a in range(2)
+    ]
+
     def give(out):
         for a in range(2):
             for part in range(parts):
-                coupled_ref[0, a, :, pl.ds(part * LANES, LANES)] = out[
+                velocity[a, :, pl.ds(part * LANES, LANES)] = out[
                     part * padded : part * padded + rows, a * LANES : (a + 1) * LANES
                 ]
+            stores[4 + a].start()
 
     def sent(count):
         for slot in range(count):
@@ -337,7 +350,8 @@
             out = centre - atmos_step * (
                 2.0 * (east * along_x + north * along_y) + 4.0 * viscosity * stiff
             )
-            new_ref[0, s] = out[:rows]
+            state[s] = out[:rows]
+            stores[s].start()
         give(total(5))
         sent(5)
 
@@ -367,7 +381,8 @@
             base.append(step)
         for s in (1, 3):
             u = fields[s, :, pl.ds(0, width)]
-            new_ref[0, s] = (u + m_centre * (ocean_step * base[s]))[:rows]
+            state[s] = (u + m_centre * (ocean_step * base[s]))[:rows]
+            stores[s].start()
         out = total(5 * ocean)
         give(out)
         for a, coef in ((0, heat_coef), (1, salt_coef)):
@@ -381,8 +396,16 @@
                 1,
             )
             step = base[s] + coef * (surface - u)
-            new_ref[0, s] = (u + m_centre * (ocean_step * step))[:rows]
+            state[s] = (u + m_centre * (ocean_step * step))[:rows]
+            stores[s].start()
         sent(5 * ocean)
+
+    for copy in stores:
+        copy.wait()
+
+
+def by_row(array):
+    return array.transpose(0, 2, 1, 3)
 
 
 def local(sizes, *arrays):
@@ -392,18 +415,21 @@
     span = parts * padded
     chunks = -(-margins // CHUNK)
     roomy = -(-margins // LANES) * LANES
-    state, velocity, wet = arrays[:3]
+    arrays = tuple(by_row(array) for array in arrays[:2]) + arrays[2:]
+    state, velocity = arrays[:2]
     slots = 5 * (comps - 1)
-    return pl.pallas_call(
+    new, coupled = pl.pallas_call(
         functools.partial(kernel, sizes),
         out_shape=(
             jax.ShapeDtypeStruct(state.shape, jnp.float32),
             jax.ShapeDtypeStruct(velocity.shape, jnp.float32),
         ),
         in_specs=[pl.BlockSpec(memory_space=pl.ANY)] * len(arrays),
-        out_specs=(pl.BlockSpec(memory_space=pltpu.VMEM),) * 2,
+        out_specs=(pl.BlockSpec(memory_space=pl.ANY),) * 2,
         scratch_shapes=[
-            *[pltpu.VMEM(array.shape, array.dtype) for array in arrays[:6]],
+            pltpu.VMEM((4, rows, width), jnp.float32),
+            pltpu.VMEM((2, rows, width), jnp.float32),
+            *[pltpu.VMEM(array.shape, array.dtype) for array in arrays[2:6]],
             pltpu.VMEM(arrays[6].shape[2:], jnp.bfloat16),
             pltpu.VMEM((span, 2 * LANES), jnp.float32),
             pltpu.VMEM((roomy, 2 * LANES), jnp.float32),
@@ -413,7 +439,7 @@
             pltpu.VMEM((2, padded, LANES), jnp.float32),
             pltpu.VMEM((slots, span, 2 * LANES), jnp.float32),
             pltpu.VMEM((slots, span, 2 * LANES), jnp.float32),
-            pltpu.SemaphoreType.DMA((6,)),
+            pltpu.SemaphoreType.DMA((10,)),
             pltpu.SemaphoreType.DMA((chunks,)),
             pltpu.SemaphoreType.DMA((slots,)),
             pltpu.SemaphoreType.DMA((slots,)),
@@ -424,6 +450,7 @@
             collective_id=0, has_side_effects=True, vmem_limit_bytes=56 * 2**20
         ),
     )(*arrays)
+    return by_row(new), by_row(coupled)
 
 
 def solution(mesh):

time: 33.8 us -> 30.6 us (0.905)
  local copies, waits for them, and re-layouts: 6.48 us -> 3.17 us
    pallas_call x2 -> x0, local copies, waits for them, and re-layouts: 3.33 us -> none  [local(): pl.pallas_call(functools.partial(kernel, sizes), out_shape=(jax.ShapeDtyp...]
where the time goes in v1:
time: 30.6 us; the launch traced here: 30.4 us
  Pallas kernels  26.6 us (87%)
  local copies, waits for them, and re-layouts  3.17 us (10%)
  between operations  0.64 us (2%)
    pallas_call x1, Pallas kernels, local(): pl.pallas_call(functools.partial(kernel, sizes), out_shape=(jax.ShapeDtyp...  26.6 us
    unnamed x2, local copies, waits for them, and re-layouts  3.17 us

profile of v1, /device:TPU:1, one launch (start us, length us, event | category | flops | bytes accessed | tf_op | source)
XLA Modules:
  0.0 30.4 jit_solution(5631363455407779591)
XLA Ops:
  0.6 26.6 %shard_map.86 = (f32[1,31,4,384]{3,2,1,0:T(4,128)}, f32[1,31,2,384]{3,2,1,0:T(2,128)}) custom-call(f32[1,31,4,384]{3,2,1,0:T(4,128)} %bitcast.5, f32[1,31,2,384]{3,2,1,0:T(2,128)} %bitcast.6, s32[31,384]{1,0:T(8,128)} %wet_hbm.1, s32[1,1,279]{2,1,0:T(1,128)} %source_hbm.1, s32[1,1,279]{2,1,0:T(1,128)} %dest_hbm.1, s32[1,1,279]{2,1,0:T(1,128)} %block_hbm.1, ...), custom_call_target="tpu_custom_call" | custom-call | tf_op jit(solution)/shard_map/pallas_call | solution.py:421
  27.2 1.6 %copy.11 = f32[1,4,31,384]{3,1,2,0:T(4,128)} copy(f32[1,4,31,384]{3,1,2,0:T(4,128)} %bitcast.4) | data formatting | bytes 380928
  28.9 1.6 %copy.12 = f32[1,2,31,384]{3,1,2,0:T(2,128)} copy(f32[1,2,31,384]{3,1,2,0:T(2,128)} %bitcast.7) | data formatting | bytes 190464

commit v2 on v1

--- a/solution.py
+++ b/solution.py
@@ -70,8 +70,8 @@
     dest_hbm,
     block_hbm,
     weight_hbm,
-    new_hbm,
-    coupled_hbm,
+    new,
+    coupled,
     state,
     velocity,
     wet,
@@ -300,21 +300,12 @@
             out = inbox[slot] if out is None else out + inbox[slot]
         return out
 
-    stores = [
-        pltpu.make_async_copy(state.at[s], new_hbm.at[0, :, s, :], load_sem.at[s])
-        for s in range(4)
-    ] + [
-        pltpu.make_async_copy(velocity.at[a], coupled_hbm.at[0, :, a, :], load_sem.at[4 + a])
-        for a in range(2)
-    ]
-
     def give(out):
         for a in range(2):
             for part in range(parts):
-                velocity[a, :, pl.ds(part * LANES, LANES)] = out[
+                coupled[a, :, pl.ds(part * LANES, LANES)] = out[
                     part * padded : part * padded + rows, a * LANES : (a + 1) * LANES
                 ]
-            stores[4 + a].start()
 
     def sent(count):
         for slot in range(count):
@@ -350,8 +341,7 @@
             out = centre - atmos_step * (
                 2.0 * (east * along_x + north * along_y) + 4.0 * viscosity * stiff
             )
-            state[s] = out[:rows]
-            stores[s].start()
+            new[s] = out[:rows]
         give(total(5))
         sent(5)
 
@@ -381,8 +371,7 @@
             base.append(step)
         for s in (1, 3):
             u = fields[s, :, pl.ds(0, width)]
-            state[s] = (u + m_centre * (ocean_step * base[s]))[:rows]
-            stores[s].start()
+            new[s] = (u + m_centre * (ocean_step * base[s]))[:rows]
         out = total(5 * ocean)
         give(out)
         for a, coef in ((0, heat_coef), (1, salt_coef)):
@@ -396,10 +385,26 @@
                 1,
             )
             step = base[s] + coef * (surface - u)
-            state[s] = (u + m_centre * (ocean_step * step))[:rows]
-            stores[s].start()
+            new[s] = (u + m_centre * (ocean_step * step))[:rows]
         sent(5 * ocean)
 
+
+def write(new_in, coupled_in, new_hbm, coupled_hbm, sem, new, coupled, load_sem):
+    loads = [
+        pltpu.make_async_copy(src.at[s], dst.at[s], load_sem.at[i, s])
+        for i, (src, dst) in enumerate(((new_in, new), (coupled_in, coupled)))
+        for s in range(src.shape[0])
+    ]
+    for copy in loads:
+        copy.start()
+    stores = [
+        pltpu.make_async_copy(slabs.at[s], out.at[0, :, s, :], sem.at[i, s])
+        for i, (slabs, out) in enumerate(((new, new_hbm), (coupled, coupled_hbm)))
+        for s in range(slabs.shape[0])
+    ]
+    for load, copy in zip(loads, stores):
+        load.wait()
+        copy.start()
     for copy in stores:
         copy.wait()
 
@@ -421,11 +426,11 @@
     new, coupled = pl.pallas_call(
         functools.partial(kernel, sizes),
         out_shape=(
-            jax.ShapeDtypeStruct(state.shape, jnp.float32),
-            jax.ShapeDtypeStruct(velocity.shape, jnp.float32),
+            jax.ShapeDtypeStruct((4, rows, width), jnp.float32),
+            jax.ShapeDtypeStruct((2, rows, width), jnp.float32),
         ),
         in_specs=[pl.BlockSpec(memory_space=pl.ANY)] * len(arrays),
-        out_specs=(pl.BlockSpec(memory_space=pl.ANY),) * 2,
+        out_specs=(pl.BlockSpec(memory_space=pltpu.VMEM),) * 2,
         scratch_shapes=[
             pltpu.VMEM((4, rows, width), jnp.float32),
             pltpu.VMEM((2, rows, width), jnp.float32),
@@ -450,6 +455,21 @@
             collective_id=0, has_side_effects=True, vmem_limit_bytes=56 * 2**20
         ),
     )(*arrays)
+    new, coupled = pl.pallas_call(
+        write,
+        out_shape=(
+            jax.ShapeDtypeStruct(state.shape, jnp.float32),
+            jax.ShapeDtypeStruct(velocity.shape, jnp.float32),
+        ),
+        in_specs=[pl.BlockSpec(memory_space=pl.ANY)] * 2,
+        out_specs=(pl.BlockSpec(memory_space=pl.ANY),) * 2,
+        scratch_shapes=[
+            pltpu.SemaphoreType.DMA((2, 4)),
+            pltpu.VMEM((4, rows, width), jnp.float32),
+            pltpu.VMEM((2, rows, width), jnp.float32),
+            pltpu.SemaphoreType.DMA((2, 4)),
+        ],
+    )(new, coupled)
     return by_row(new), by_row(coupled)
 
 

time: 30.6 us -> 29.1 us (0.951)
  local copies, waits for them, and re-layouts: 3.17 us -> 0 us
  Pallas kernels: 26.6 us -> 28.3 us
    unnamed x2 -> x0, local copies, waits for them, and re-layouts: 3.17 us -> none
    pallas_call x0 -> x1, Pallas kernels: none -> 1.67 us  [local(): pl.pallas_call(write, out_shape=(jax.ShapeDtypeStruct(state.shape, jnp.fl...]
where the time goes in v2:
time: 29.1 us; the launch traced here: 29 us
  Pallas kernels  28.3 us (97%)
  between operations  0.64 us (2%)
    pallas_call x1, Pallas kernels, local(): pl.pallas_call(functools.partial(kernel, sizes), out_shape=(jax.ShapeDtyp...  26.7 us
    pallas_call x1, Pallas kernels, local(): pl.pallas_call(write, out_shape=(jax.ShapeDtypeStruct(state.shape, jnp.fl...  1.67 us

profile of v2, /device:TPU:1, one launch (start us, length us, event | category | flops | bytes accessed | tf_op | source)
XLA Modules:
  0.0 29.0 jit_solution(16696883750011182840)
XLA Ops:
  0.6 26.7 %shard_map.86 = (f32[4,31,384]{2,1,0:T(8,128)}, f32[2,31,384]{2,1,0:T(8,128)}) custom-call(f32[1,31,4,384]{3,2,1,0:T(4,128)} %bitcast.4, f32[1,31,2,384]{3,2,1,0:T(2,128)} %bitcast.5, s32[31,384]{1,0:T(8,128)} %wet_hbm.1, s32[1,1,279]{2,1,0:T(1,128)} %source_hbm.1, s32[1,1,279]{2,1,0:T(1,128)} %dest_hbm.1, s32[1,1,279]{2,1,0:T(1,128)} %block_hbm.1, ...), custom_call_target="tpu_custom_call" | custom-call | tf_op jit(solution)/shard_map/pallas_call | solution.py:426
  27.3 1.7 %shard_map.87 = (f32[1,31,4,384]{3,2,1,0:T(4,128)}, f32[1,31,2,384]{3,2,1,0:T(2,128)}) custom-call(f32[4,31,384]{2,1,0:T(8,128)} %get-tuple-element.6.new_in, f32[2,31,384]{2,1,0:T(8,128)} %get-tuple-element.7.coupled_in), custom_call_target="tpu_custom_call" | custom-call | tf_op jit(solution)/shard_map/pallas_call | solution.py:458

commit v3 on v2

--- a/solution.py
+++ b/solution.py
@@ -82,6 +82,7 @@
     payload,
     picked,
     pieces,
+    onehot,
     fields,
     strips,
     edges,
@@ -204,6 +205,31 @@
     strips[0] = right_going
     strips[1] = left_going
 
+    loads[3].wait()
+    loads[4].wait()
+    target = dest[0]
+    offset = (target & (tiles - 1)) - tile + 2
+    offset = jnp.where(offset < 0, offset + tiles, offset)
+    offset = jnp.where(offset >= tiles, offset - tiles, offset)
+    place = place_of(block[0])
+    codes = offset * span + place
+    codes = jnp.where(me == ocean, (target >> 5) * (5 * span) + codes, codes)
+    numbers = lax.broadcasted_iota(jnp.int32, (span, margins), 0)
+
+    def mark(slot):
+        onehot[pl.ds(slot * span, span), pl.ds(0, margins)] = (
+            (numbers == codes - slot * span).astype(jnp.float32).astype(jnp.bfloat16)
+        )
+
+    onehot[...] = jnp.zeros_like(onehot)
+    for slot in range(5):
+        mark(slot)
+
+    @pl.when(me == ocean)
+    def _():
+        for slot in range(5, 5 * ocean):
+            mark(slot)
+
     rank = lax.rem(lax.broadcasted_iota(jnp.int32, (2 * GROUP, LANES), 0), GROUP)
     for (low, high), copy in zip(bounds, chunks):
         copy.wait()
@@ -225,23 +251,15 @@
                     a * GROUP : a * GROUP + count
                 ]
 
-    loads[3].wait()
-    loads[4].wait()
-    target = dest[0]
-    offset = (target & (tiles - 1)) - tile + 2
-    offset = jnp.where(offset < 0, offset + tiles, offset)
-    offset = jnp.where(offset >= tiles, offset - tiles, offset)
-    place = place_of(block[0])
     whole = pieces[...]
     coarse = whole.astype(jnp.bfloat16)
     fine = (whole - coarse.astype(jnp.float32)).astype(jnp.bfloat16)
 
-    def gathered(codes, low, count):
-        numbers = lax.broadcasted_iota(jnp.int32, (count, margins), 0) + low
-        onehot = (numbers == codes).astype(jnp.float32).astype(jnp.bfloat16)
-        return jnp.dot(
-            onehot, coarse[:margins], preferred_element_type=jnp.float32
-        ) + jnp.dot(onehot, fine[:margins], preferred_element_type=jnp.float32)
+    def gathered(low, count):
+        held = onehot[pl.ds(low, count), :]
+        return jnp.dot(held, coarse, preferred_element_type=jnp.float32) + jnp.dot(
+            held, fine, preferred_element_type=jnp.float32
+        )
 
     def message(slot, far_slot, comp, k):
         return pltpu.make_async_remote_copy(
@@ -266,19 +284,17 @@
     @pl.when(me == ocean)
     def _():
         pl.semaphore_wait(barrier, 2 + 5 * ocean)
-        codes = (offset * ocean + (target >> 5)) * span + place
+        order = [(comp, k) for k in OFFSETS for comp in range(ocean - 1)]
+        for comp, k in order + [(ocean - 1, k) for k in OFFSETS]:
+            slot = comp * 5 + k
+            outbox[slot] = gathered(slot * span, span)
+            message(slot, k, comp, k).start()
+
+    @pl.when(me != ocean)
+    def _():
+        pl.semaphore_wait(barrier, 2 + 5)
         for k in OFFSETS:
-            out = gathered(codes, k * ocean * span, ocean * span)
-            for comp in range(ocean):
-                outbox[comp * 5 + k] = out[comp * span : (comp + 1) * span]
-                message(comp * 5 + k, k, comp, k).start()
-
-    @pl.when(me != ocean)
-    def _():
-        pl.semaphore_wait(barrier, 2 + 5)
-        codes = offset * span + place
-        for k in OFFSETS:
-            outbox[k] = gathered(codes, k * span, span)
+            outbox[k] = gathered(k * span, span)
             message(k, me * 5 + k, ocean, k).start()
 
     for side in range(2):
@@ -389,21 +405,13 @@
         sent(5 * ocean)
 
 
-def write(new_in, coupled_in, new_hbm, coupled_hbm, sem, new, coupled, load_sem):
-    loads = [
-        pltpu.make_async_copy(src.at[s], dst.at[s], load_sem.at[i, s])
-        for i, (src, dst) in enumerate(((new_in, new), (coupled_in, coupled)))
-        for s in range(src.shape[0])
-    ]
-    for copy in loads:
-        copy.start()
+def write(new, coupled, new_hbm, coupled_hbm, sem):
     stores = [
         pltpu.make_async_copy(slabs.at[s], out.at[0, :, s, :], sem.at[i, s])
         for i, (slabs, out) in enumerate(((new, new_hbm), (coupled, coupled_hbm)))
         for s in range(slabs.shape[0])
     ]
-    for load, copy in zip(loads, stores):
-        load.wait()
+    for copy in stores:
         copy.start()
     for copy in stores:
         copy.wait()
@@ -426,8 +434,8 @@
     new, coupled = pl.pallas_call(
         functools.partial(kernel, sizes),
         out_shape=(
-            jax.ShapeDtypeStruct((4, rows, width), jnp.float32),
-            jax.ShapeDtypeStruct((2, rows, width), jnp.float32),
+            pltpu.VMEM((4, rows, width), jnp.float32),
+            pltpu.VMEM((2, rows, width), jnp.float32),
         ),
         in_specs=[pl.BlockSpec(memory_space=pl.ANY)] * len(arrays),
         out_specs=(pl.BlockSpec(memory_space=pltpu.VMEM),) * 2,
@@ -439,6 +447,7 @@
             pltpu.VMEM((span, 2 * LANES), jnp.float32),
             pltpu.VMEM((roomy, 2 * LANES), jnp.float32),
             pltpu.VMEM((roomy, 2 * LANES), jnp.float32),
+            pltpu.VMEM((slots * span, roomy), jnp.bfloat16),
             pltpu.VMEM((7, padded, width + LANES), jnp.float32),
             pltpu.VMEM((2, padded, LANES), jnp.float32),
             pltpu.VMEM((2, padded, LANES), jnp.float32),
@@ -461,14 +470,10 @@
             jax.ShapeDtypeStruct(state.shape, jnp.float32),
             jax.ShapeDtypeStruct(velocity.shape, jnp.float32),
         ),
-        in_specs=[pl.BlockSpec(memory_space=pl.ANY)] * 2,
+        in_specs=[pl.BlockSpec(memory_space=pltpu.VMEM)] * 2,
         out_specs=(pl.BlockSpec(memory_space=pl.ANY),) * 2,
-        scratch_shapes=[
-            pltpu.SemaphoreType.DMA((2, 4)),
-            pltpu.VMEM((4, rows, width), jnp.float32),
-            pltpu.VMEM((2, rows, width), jnp.float32),
-            pltpu.SemaphoreType.DMA((2, 4)),
-        ],
+        scratch_shapes=[pltpu.SemaphoreType.DMA((2, 4))],
+        compiler_params=pltpu.CompilerParams(vmem_limit_bytes=2**20),
     )(new, coupled)
     return by_row(new), by_row(coupled)
 

time: 29.1 us -> 26.3 us (0.904)
  Pallas kernels: 28.3 us -> 25.5 us
    pallas_call x1, Pallas kernels: 26.7 us -> 24.7 us  [local(): pl.pallas_call(functools.partial(kernel, sizes), out_shape=(pltpu.VMEM((4...]
    pallas_call x1, Pallas kernels: 1.67 us -> 0.77 us  [local(): pl.pallas_call(write, out_shape=(jax.ShapeDtypeStruct(state.shape, jnp.fl...]
where the time goes in v3:
time: 26.3 us; the launch traced here: 26.1 us
  Pallas kernels  25.5 us (97%)
  between operations  0.64 us (2%)
    pallas_call x1, Pallas kernels, local(): pl.pallas_call(functools.partial(kernel, sizes), out_shape=(pltpu.VMEM((4...  24.7 us
    pallas_call x1, Pallas kernels, local(): pl.pallas_call(write, out_shape=(jax.ShapeDtypeStruct(state.shape, jnp.fl...  0.77 us

profile of v3, /device:TPU:1, one launch (start us, length us, event | category | flops | bytes accessed | tf_op | source)
XLA Modules:
  0.0 26.1 jit_solution(1130816198091388361)
XLA Ops:
  0.6 24.7 %shard_map.86 = (f32[4,31,384]{2,1,0:T(8,128)S(1)}, f32[2,31,384]{2,1,0:T(8,128)S(1)}) custom-call(f32[1,31,4,384]{3,2,1,0:T(4,128)} %bitcast.4, f32[1,31,2,384]{3,2,1,0:T(2,128)} %bitcast.5, s32[31,384]{1,0:T(8,128)} %wet_hbm.1, s32[1,1,279]{2,1,0:T(1,128)} %source_hbm.1, s32[1,1,279]{2,1,0:T(1,128)} %dest_hbm.1, s32[1,1,279]{2,1,0:T(1,128)} %block_hbm.1, ...), custom_call_target="tpu_custom_call" | custom-call | tf_op jit(solution)/shard_map/pallas_call | solution.py:434
  25.4 0.8 %shard_map.87 = (f32[1,31,4,384]{3,2,1,0:T(4,128)}, f32[1,31,2,384]{3,2,1,0:T(2,128)}) custom-call(f32[4,31,384]{2,1,0:T(8,128)S(1)} %get-tuple-element.6.new, f32[2,31,384]{2,1,0:T(8,128)S(1)} %get-tuple-element.7.coupled), custom_call_target="tpu_custom_call" | custom-call | tf_op jit(solution)/shard_map/pallas_call | solution.py:467

commit v4 on v3

--- a/solution.py
+++ b/solution.py
@@ -157,7 +157,7 @@
         )
         for i, (low, high) in enumerate(bounds)
     ]
-    for copy in loads[:5] + chunks + loads[5:]:
+    for copy in loads + chunks:
         copy.start()
 
     payload[...] = jnp.zeros_like(payload)
@@ -185,26 +185,6 @@
         preferred_element_type=jnp.float32,
     )
 
-    for copy in loads[5:]:
-        copy.wait()
-    for s in range(4):
-        fields[s, pl.ds(0, rows), pl.ds(0, width)] = state[s]
-    fields[4, pl.ds(0, rows), pl.ds(0, width)] = velocity[0]
-    fields[5, pl.ds(0, rows), pl.ds(0, width)] = wet[...].astype(jnp.float32)
-    fields[6, pl.ds(0, rows), pl.ds(0, width)] = velocity[1]
-    for s in range(7):
-        fields[s, pl.ds(rows, 1), pl.ds(0, width)] = jnp.zeros((1, width), jnp.float32)
-    lane = lax.broadcasted_iota(jnp.int32, (padded, LANES), 1)
-    right_going = fields[0, :, pl.ds(width - LANES, LANES)]
-    left_going = fields[0, :, pl.ds(0, LANES)]
-    for s in range(1, 6):
-        moved = pltpu.roll(fields[s, :, pl.ds(width - LANES, LANES)], LANES - 4 * s, 1)
-        right_going = jnp.where(lane < LANES - 4 * s, moved, right_going)
-        moved = pltpu.roll(fields[s, :, pl.ds(0, LANES)], 4 * s, 1)
-        left_going = jnp.where(lane >= 4 * s, moved, left_going)
-    strips[0] = right_going
-    strips[1] = left_going
-
     loads[3].wait()
     loads[4].wait()
     target = dest[0]
@@ -221,18 +201,37 @@
             (numbers == codes - slot * span).astype(jnp.float32).astype(jnp.bfloat16)
         )
 
+    lane = lax.broadcasted_iota(jnp.int32, (padded, LANES), 1)
+
+    def take_fields():
+        for copy in loads[5:]:
+            copy.wait()
+        for s in range(4):
+            fields[s, pl.ds(0, rows), pl.ds(0, width)] = state[s]
+        fields[4, pl.ds(0, rows), pl.ds(0, width)] = velocity[0]
+        fields[5, pl.ds(0, rows), pl.ds(0, width)] = wet[...].astype(jnp.float32)
+        fields[6, pl.ds(0, rows), pl.ds(0, width)] = velocity[1]
+        for s in range(7):
+            fields[s, pl.ds(rows, 1), pl.ds(0, width)] = jnp.zeros((1, width), jnp.float32)
+        right_going = fields[0, :, pl.ds(width - LANES, LANES)]
+        left_going = fields[0, :, pl.ds(0, LANES)]
+        for s in range(1, 6):
+            moved = pltpu.roll(fields[s, :, pl.ds(width - LANES, LANES)], LANES - 4 * s, 1)
+            right_going = jnp.where(lane < LANES - 4 * s, moved, right_going)
+            moved = pltpu.roll(fields[s, :, pl.ds(0, LANES)], 4 * s, 1)
+            left_going = jnp.where(lane >= 4 * s, moved, left_going)
+        strips[0] = right_going
+        strips[1] = left_going
+
+    rank = lax.rem(lax.broadcasted_iota(jnp.int32, (2 * GROUP, LANES), 0), GROUP)
     onehot[...] = jnp.zeros_like(onehot)
-    for slot in range(5):
-        mark(slot)
-
-    @pl.when(me == ocean)
-    def _():
-        for slot in range(5, 5 * ocean):
+    per_chunk = -(-5 * ocean // (len(bounds) - 2))
+    for i, ((low, high), copy) in enumerate(zip(bounds, chunks)):
+        copy.wait()
+        for slot in range(i * per_chunk, min((i + 1) * per_chunk, 5 * ocean)):
             mark(slot)
-
-    rank = lax.rem(lax.broadcasted_iota(jnp.int32, (2 * GROUP, LANES), 0), GROUP)
-    for (low, high), copy in zip(bounds, chunks):
-        copy.wait()
+        if i == len(bounds) - 2:
+            take_fields()
         for first in range(low, high, GROUP):
             count = min(GROUP, high - first)
             held = jnp.concatenate(
@@ -284,7 +283,9 @@
     @pl.when(me == ocean)
     def _():
         pl.semaphore_wait(barrier, 2 + 5 * ocean)
-        order = [(comp, k) for k in OFFSETS for comp in range(ocean - 1)]
+        for side in range(2):
+            strip(side).start()
+        order = [(comp, k) for k in OFFSETS for comp in reversed(range(ocean - 1))]
         for comp, k in order + [(ocean - 1, k) for k in OFFSETS]:
             slot = comp * 5 + k
             outbox[slot] = gathered(slot * span, span)
@@ -293,12 +294,12 @@
     @pl.when(me != ocean)
     def _():
         pl.semaphore_wait(barrier, 2 + 5)
+        for side in range(2):
+            strip(side).start()
         for k in OFFSETS:
             outbox[k] = gathered(k * span, span)
             message(k, me * 5 + k, ocean, k).start()
 
-    for side in range(2):
-        strip(side).start()
     for side in range(2):
         strip(side).wait()
 
@@ -311,7 +312,7 @@
 
     def total(count):
         out = None
-        for slot in range(count):
+        for slot in [comp * 5 + k for k in OFFSETS for comp in range(count // 5)]:
             pltpu.make_async_copy(inbox.at[slot], inbox.at[slot], in_sem.at[slot]).wait()
             out = inbox[slot] if out is None else out + inbox[slot]
         return out

time: 26.3 us -> 24.5 us (0.932)
  the two profiles are of different devices: /device:TPU:1 before, /device:TPU:0 now
where the time goes in v4:
time: 24.5 us; the launch traced here: 24.3 us
  Pallas kernels  23.7 us (97%)
  between operations  0.64 us (3%)
    pallas_call x1, Pallas kernels, local(): pl.pallas_call(functools.partial(kernel, sizes), out_shape=(pltpu.VMEM((4...  22.9 us
    pallas_call x1, Pallas kernels, local(): pl.pallas_call(write, out_shape=(jax.ShapeDtypeStruct(state.shape, jnp.fl...  0.77 us

profile of v4, /device:TPU:0, one launch (start us, length us, event | category | flops | bytes accessed | tf_op | source)
XLA Modules:
  0.0 24.3 jit_solution(5002741534663160874)
XLA Ops:
  0.6 22.9 %shard_map.86 = (f32[4,31,384]{2,1,0:T(8,128)S(1)}, f32[2,31,384]{2,1,0:T(8,128)S(1)}) custom-call(f32[1,31,4,384]{3,2,1,0:T(4,128)} %bitcast.4, f32[1,31,2,384]{3,2,1,0:T(2,128)} %bitcast.5, s32[31,384]{1,0:T(8,128)} %wet_hbm.1, s32[1,1,279]{2,1,0:T(1,128)} %source_hbm.1, s32[1,1,279]{2,1,0:T(1,128)} %dest_hbm.1, s32[1,1,279]{2,1,0:T(1,128)} %block_hbm.1, ...), custom_call_target="tpu_custom_call" | custom-call | tf_op jit(solution)/shard_map/pallas_call | solution.py:435
  23.6 0.8 %shard_map.87 = (f32[1,31,4,384]{3,2,1,0:T(4,128)}, f32[1,31,2,384]{3,2,1,0:T(2,128)}) custom-call(f32[4,31,384]{2,1,0:T(8,128)S(1)} %get-tuple-element.6.new, f32[2,31,384]{2,1,0:T(8,128)S(1)} %get-tuple-element.7.coupled), custom_call_target="tpu_custom_call" | custom-call | tf_op jit(solution)/shard_map/pallas_call | solution.py:468

commit v5 on v4

--- a/solution.py
+++ b/solution.py
@@ -21,7 +21,7 @@
 LANES = 128
 GROUP = 8
 CHUNK = 40
-OFFSETS = (0, 4, 1, 3, 2)
+OFFSETS = (0, 3, 1, 4, 2)
 
 
 def gll_tables():
@@ -117,20 +117,6 @@
             barrier, inc=1, device_id=device(comp, step), device_id_type=MESH
         )
 
-    greet(me, -1)
-    greet(me, 1)
-
-    @pl.when(me == ocean)
-    def _():
-        for k in range(5):
-            for comp in range(ocean):
-                greet(comp, k - 2)
-
-    @pl.when(me != ocean)
-    def _():
-        for k in range(5):
-            greet(ocean, k - 2)
-
     loads = [
         pltpu.make_async_copy(src, dst, load_sem.at[i])
         for i, (src, dst) in enumerate(
@@ -148,17 +134,32 @@
             )
         )
     ]
-    bounds = [(low, min(low + CHUNK, margins)) for low in range(0, margins, CHUNK)]
-    chunks = [
-        pltpu.make_async_copy(
-            weight_hbm.at[0, 0, pl.ds(low, high - low)],
-            weight.at[pl.ds(low, high - low)],
+
+    def chunk(i, count):
+        return pltpu.make_async_copy(
+            weight_hbm.at[0, 0, pl.ds(i * CHUNK, count)],
+            weight.at[pl.ds(i * CHUNK, count)],
             chunk_sem.at[i],
         )
-        for i, (low, high) in enumerate(bounds)
-    ]
-    for copy in loads + chunks:
+
+    for copy in loads:
         copy.start()
+    for low in range(0, margins, CHUNK):
+        chunk(low // CHUNK, min(CHUNK, margins - low)).start()
+
+    greet(me, -1)
+    greet(me, 1)
+
+    @pl.when(me == ocean)
+    def _():
+        for k in range(5):
+            for comp in range(ocean):
+                greet(comp, k - 2)
+
+    @pl.when(me != ocean)
+    def _():
+        for k in range(5):
+            greet(ocean, k - 2)
 
     payload[...] = jnp.zeros_like(payload)
     pieces[pl.ds(margins // 8 * 8, pieces.shape[0] - margins // 8 * 8), :] = jnp.zeros(
@@ -197,7 +198,7 @@
     numbers = lax.broadcasted_iota(jnp.int32, (span, margins), 0)
 
     def mark(slot):
-        onehot[pl.ds(slot * span, span), pl.ds(0, margins)] = (
+        onehot[pl.ds(pl.multiple_of(slot * span, span), span), pl.ds(0, margins)] = (
             (numbers == codes - slot * span).astype(jnp.float32).astype(jnp.bfloat16)
         )
 
@@ -224,31 +225,40 @@
         strips[1] = left_going
 
     rank = lax.rem(lax.broadcasted_iota(jnp.int32, (2 * GROUP, LANES), 0), GROUP)
-    onehot[...] = jnp.zeros_like(onehot)
-    per_chunk = -(-5 * ocean // (len(bounds) - 2))
-    for i, ((low, high), copy) in enumerate(zip(bounds, chunks)):
-        copy.wait()
-        for slot in range(i * per_chunk, min((i + 1) * per_chunk, 5 * ocean)):
-            mark(slot)
-        if i == len(bounds) - 2:
-            take_fields()
-        for first in range(low, high, GROUP):
-            count = min(GROUP, high - first)
+    def multiply(low, count):
+        for first in range(0, count, GROUP):
+            here = min(GROUP, count - first)
             held = jnp.concatenate(
-                [picked[pl.ds(first, GROUP), pl.ds(a * LANES, LANES)] for a in range(2)], 0
+                [picked[pl.ds(low + first, GROUP), pl.ds(a * LANES, LANES)] for a in range(2)], 0
             )
             spread = jnp.concatenate(
-                [jnp.where(rank == i, held, 0.0).astype(jnp.bfloat16) for i in range(count)], 1
+                [jnp.where(rank == i, held, 0.0).astype(jnp.bfloat16) for i in range(here)], 1
             )
             product = jnp.dot(
                 spread,
-                weight[pl.ds(first, count)].reshape(count * LANES, LANES),
+                weight[pl.ds(low + first, here)].reshape(here * LANES, LANES),
                 preferred_element_type=jnp.float32,
             )
             for a in range(2):
-                pieces[pl.ds(first, count), pl.ds(a * LANES, LANES)] = product[
-                    a * GROUP : a * GROUP + count
+                pieces[pl.ds(low + first, here), pl.ds(a * LANES, LANES)] = product[
+                    a * GROUP : a * GROUP + here
                 ]
+
+    onehot[...] = jnp.zeros_like(onehot)
+    full = margins // CHUNK
+    marks = onehot.shape[0] // span // full
+
+    def work(i, carry):
+        chunk(i, CHUNK).wait()
+        for j in range(marks):
+            mark(i * marks + j)
+        multiply(pl.multiple_of(i * CHUNK, CHUNK), CHUNK)
+        return carry
+
+    lax.fori_loop(0, full, work, 0)
+    take_fields()
+    chunk(full, margins - full * CHUNK).wait()
+    multiply(full * CHUNK, margins - full * CHUNK)
 
     whole = pieces[...]
     coarse = whole.astype(jnp.bfloat16)
@@ -280,25 +290,29 @@
             device_id_type=MESH,
         )
 
+    at_sea = me // ocean
+
     @pl.when(me == ocean)
     def _():
         pl.semaphore_wait(barrier, 2 + 5 * ocean)
-        for side in range(2):
-            strip(side).start()
-        order = [(comp, k) for k in OFFSETS for comp in reversed(range(ocean - 1))]
-        for comp, k in order + [(ocean - 1, k) for k in OFFSETS]:
-            slot = comp * 5 + k
-            outbox[slot] = gathered(slot * span, span)
-            message(slot, k, comp, k).start()
 
     @pl.when(me != ocean)
     def _():
         pl.semaphore_wait(barrier, 2 + 5)
-        for side in range(2):
-            strip(side).start()
+
+    for side in range(2):
+        strip(side).start()
+
+    def send(turn, carry):
+        band = (2 * turn + 1) % ocean
+        comp = at_sea * band + (1 - at_sea) * ocean
         for k in OFFSETS:
-            outbox[k] = gathered(k * span, span)
-            message(k, me * 5 + k, ocean, k).start()
+            slot = at_sea * band * 5 + k
+            outbox[slot] = gathered(pl.multiple_of(slot * span, span), span)
+            message(slot, (1 - at_sea) * me * 5 + k, comp, k).start()
+        return carry
+
+    lax.fori_loop(0, 1 + at_sea * (ocean - 1), send, 0)
 
     for side in range(2):
         strip(side).wait()
@@ -428,6 +442,7 @@
     padded = rows + 1
     span = parts * padded
     chunks = -(-margins // CHUNK)
+    full = margins // CHUNK
     roomy = -(-margins // LANES) * LANES
     arrays = tuple(by_row(array) for array in arrays[:2]) + arrays[2:]
     state, velocity = arrays[:2]
@@ -448,7 +463,7 @@
             pltpu.VMEM((span, 2 * LANES), jnp.float32),
             pltpu.VMEM((roomy, 2 * LANES), jnp.float32),
             pltpu.VMEM((roomy, 2 * LANES), jnp.float32),
-            pltpu.VMEM((slots * span, roomy), jnp.bfloat16),
+            pltpu.VMEM((-(-slots // full) * full * span, roomy), jnp.bfloat16),
             pltpu.VMEM((7, padded, width + LANES), jnp.float32),
             pltpu.VMEM((2, padded, LANES), jnp.float32),
             pltpu.VMEM((2, padded, LANES), jnp.float32),

time: 24.5 us -> 23.2 us (0.947)
  the two profiles are of different devices: /device:TPU:0 before, /device:TPU:1 now
where the time goes in v5:
time: 23.2 us; the launch traced here: 22.8 us
  Pallas kernels  22.2 us (96%)
  between operations  0.64 us (3%)
    pallas_call x1, Pallas kernels, local(): pl.pallas_call(functools.partial(kernel, sizes), out_shape=(pltpu.VMEM((4...  21.4 us
    pallas_call x1, Pallas kernels, local(): pl.pallas_call(write, out_shape=(jax.ShapeDtypeStruct(state.shape, jnp.fl...  0.77 us

profile of v5, /device:TPU:1, one launch (start us, length us, event | category | flops | bytes accessed | tf_op | source)
XLA Modules:
  0.0 22.8 jit_solution(7482730147901242463)
XLA Ops:
  0.6 21.4 %shard_map.86 = (f32[4,31,384]{2,1,0:T(8,128)S(1)}, f32[2,31,384]{2,1,0:T(8,128)S(1)}) custom-call(f32[1,31,4,384]{3,2,1,0:T(4,128)} %bitcast.4, f32[1,31,2,384]{3,2,1,0:T(2,128)} %bitcast.5, s32[31,384]{1,0:T(8,128)} %wet_hbm.1, s32[1,1,279]{2,1,0:T(1,128)} %source_hbm.1, s32[1,1,279]{2,1,0:T(1,128)} %dest_hbm.1, s32[1,1,279]{2,1,0:T(1,128)} %block_hbm.1, ...), custom_call_target="tpu_custom_call" | custom-call | tf_op jit(solution)/shard_map/pallas_call | solution.py:450
  22.0 0.8 %shard_map.87 = (f32[1,31,4,384]{3,2,1,0:T(4,128)}, f32[1,31,2,384]{3,2,1,0:T(2,128)}) custom-call(f32[4,31,384]{2,1,0:T(8,128)S(1)} %get-tuple-element.6.new, f32[2,31,384]{2,1,0:T(8,128)S(1)} %get-tuple-element.7.coupled), custom_call_target="tpu_custom_call" | custom-call | tf_op jit(solution)/shard_map/pallas_call | solution.py:483

commit v6 on v5

--- a/solution.py
+++ b/solution.py
@@ -306,9 +306,11 @@
     def send(turn, carry):
         band = (2 * turn + 1) % ocean
         comp = at_sea * band + (1 - at_sea) * ocean
+        start = at_sea * band * 5
+        every = gathered(pl.multiple_of(start * span, span), 5 * span)
         for k in OFFSETS:
-            slot = at_sea * band * 5 + k
-            outbox[slot] = gathered(pl.multiple_of(slot * span, span), span)
+            slot = start + k
+            outbox[slot] = every[k * span : (k + 1) * span]
             message(slot, (1 - at_sea) * me * 5 + k, comp, k).start()
         return carry
 

time: 23.2 us -> 23 us (level)
  the two profiles are of different devices: /device:TPU:1 before, /device:TPU:0 now
where the time goes in v6:
time: 23 us; the launch traced here: 22.9 us
  Pallas kernels  22.2 us (97%)
  between operations  0.64 us (3%)
    pallas_call x1, Pallas kernels, local(): pl.pallas_call(functools.partial(kernel, sizes), out_shape=(pltpu.VMEM((4...  21.5 us
    pallas_call x1, Pallas kernels, local(): pl.pallas_call(write, out_shape=(jax.ShapeDtypeStruct(state.shape, jnp.fl...  0.77 us

profile of v6, /device:TPU:0, one launch (start us, length us, event | category | flops | bytes accessed | tf_op | source)
XLA Modules:
  0.0 22.9 jit_solution(15494457639932693627)
XLA Ops:
  0.6 21.5 %shard_map.86 = (f32[4,31,384]{2,1,0:T(8,128)S(1)}, f32[2,31,384]{2,1,0:T(8,128)S(1)}) custom-call(f32[1,31,4,384]{3,2,1,0:T(4,128)} %bitcast.4, f32[1,31,2,384]{3,2,1,0:T(2,128)} %bitcast.5, s32[31,384]{1,0:T(8,128)} %wet_hbm.1, s32[1,1,279]{2,1,0:T(1,128)} %source_hbm.1, s32[1,1,279]{2,1,0:T(1,128)} %dest_hbm.1, s32[1,1,279]{2,1,0:T(1,128)} %block_hbm.1, ...), custom_call_target="tpu_custom_call" | custom-call | tf_op jit(solution)/shard_map/pallas_call | solution.py:452
  22.1 0.8 %shard_map.87 = (f32[1,31,4,384]{3,2,1,0:T(4,128)}, f32[1,31,2,384]{3,2,1,0:T(2,128)}) custom-call(f32[4,31,384]{2,1,0:T(8,128)S(1)} %get-tuple-element.6.new, f32[2,31,384]{2,1,0:T(8,128)S(1)} %get-tuple-element.7.coupled), custom_call_target="tpu_custom_call" | custom-call | tf_op jit(solution)/shard_map/pallas_call | solution.py:485

commit v7 on v6

--- a/solution.py
+++ b/solution.py
@@ -121,11 +121,11 @@
         pltpu.make_async_copy(src, dst, load_sem.at[i])
         for i, (src, dst) in enumerate(
             (
+                (dest_hbm, dest),
+                (block_hbm, block),
                 (source_hbm, source),
                 (state_hbm.at[0, :, 0, :], state.at[0]),
                 (state_hbm.at[0, :, 2, :], state.at[2]),
-                (dest_hbm, dest),
-                (block_hbm, block),
                 (state_hbm.at[0, :, 1, :], state.at[1]),
                 (state_hbm.at[0, :, 3, :], state.at[3]),
                 (velocity_hbm.at[0, :, 0, :], velocity.at[0]),
@@ -165,29 +165,12 @@
     pieces[pl.ds(margins // 8 * 8, pieces.shape[0] - margins // 8 * 8), :] = jnp.zeros(
         (pieces.shape[0] - margins // 8 * 8, 2 * LANES), jnp.float32
     )
-    for copy in loads[:3]:
-        copy.wait()
-    for a in range(2):
-        for part in range(parts):
-            payload[pl.ds(part * padded, rows), pl.ds(a * LANES, LANES)] = state[
-                2 * a, :, pl.ds(part * LANES, LANES)
-            ]
-
     def place_of(numbers):
         row = (numbers * 171) >> 9
         return (numbers - 3 * row) * padded + row
 
-    slots = lax.broadcasted_iota(jnp.int32, (span, margins), 0)
-    chosen = (slots == place_of(source[0])).astype(jnp.float32)
-    picked[pl.ds(0, margins), :] = lax.dot_general(
-        chosen.T.astype(jnp.bfloat16),
-        payload[...].astype(jnp.bfloat16),
-        (((1,), (0,)), ((), ())),
-        preferred_element_type=jnp.float32,
-    )
-
-    loads[3].wait()
-    loads[4].wait()
+    loads[0].wait()
+    loads[1].wait()
     target = dest[0]
     offset = (target & (tiles - 1)) - tile + 2
     offset = jnp.where(offset < 0, offset + tiles, offset)
@@ -201,6 +184,38 @@
         onehot[pl.ds(pl.multiple_of(slot * span, span), span), pl.ds(0, margins)] = (
             (numbers == codes - slot * span).astype(jnp.float32).astype(jnp.bfloat16)
         )
+
+    last = margins // LANES * LANES
+    onehot[:, pl.ds(last, onehot.shape[1] - last)] = jnp.zeros(
+        (onehot.shape[0], onehot.shape[1] - last), jnp.bfloat16
+    )
+
+    def mark_band(band, carry):
+        for k in range(5):
+            mark(band * 5 + k)
+        return carry
+
+    lax.fori_loop(0, 1 + me // ocean * (ocean - 1), mark_band, 0)
+
+    loads[2].wait()
+    slots = lax.broadcasted_iota(jnp.int32, (span, margins), 0)
+    chosen = (slots == place_of(source[0])).astype(jnp.float32)
+    chosen = chosen.T.astype(jnp.bfloat16)
+
+    for copy in loads[3:5]:
+        copy.wait()
+    for a in range(2):
+        for part in range(parts):
+            payload[pl.ds(part * padded, rows), pl.ds(a * LANES, LANES)] = state[
+                2 * a, :, pl.ds(part * LANES, LANES)
+            ]
+
+    picked[pl.ds(0, margins), :] = lax.dot_general(
+        chosen,
+        payload[...].astype(jnp.bfloat16),
+        (((1,), (0,)), ((), ())),
+        preferred_element_type=jnp.float32,
+    )
 
     lane = lax.broadcasted_iota(jnp.int32, (padded, LANES), 1)
 
@@ -244,14 +259,10 @@
                     a * GROUP : a * GROUP + here
                 ]
 
-    onehot[...] = jnp.zeros_like(onehot)
     full = margins // CHUNK
-    marks = onehot.shape[0] // span // full
 
     def work(i, carry):
         chunk(i, CHUNK).wait()
-        for j in range(marks):
-            mark(i * marks + j)
         multiply(pl.multiple_of(i * CHUNK, CHUNK), CHUNK)
         return carry
 
@@ -444,7 +455,6 @@
     padded = rows + 1
     span = parts * padded
     chunks = -(-margins // CHUNK)
-    full = margins // CHUNK
     roomy = -(-margins // LANES) * LANES
     arrays = tuple(by_row(array) for array in arrays[:2]) + arrays[2:]
     state, velocity = arrays[:2]
@@ -465,7 +475,7 @@
             pltpu.VMEM((span, 2 * LANES), jnp.float32),
             pltpu.VMEM((roomy, 2 * LANES), jnp.float32),
             pltpu.VMEM((roomy, 2 * LANES), jnp.float32),
-            pltpu.VMEM((-(-slots // full) * full * span, roomy), jnp.bfloat16),
+            pltpu.VMEM((slots * span, roomy), jnp.bfloat16),
             pltpu.VMEM((7, padded, width + LANES), jnp.float32),
             pltpu.VMEM((2, padded, LANES), jnp.float32),
             pltpu.VMEM((2, padded, LANES), jnp.float32),

time: 23 us -> 23 us (level)
  no operation moved by 1% of the time
where the time goes in v7:
time: 23 us; the launch traced here: 22.9 us
  Pallas kernels  22.3 us (97%)
  between operations  0.64 us (3%)
    pallas_call x1, Pallas kernels, local(): pl.pallas_call(functools.partial(kernel, sizes), out_shape=(pltpu.VMEM((4...  21.5 us
    pallas_call x1, Pallas kernels, local(): pl.pallas_call(write, out_shape=(jax.ShapeDtypeStruct(state.shape, jnp.fl...  0.77 us

profile of v7, /device:TPU:0, one launch (start us, length us, event | category | flops | bytes accessed | tf_op | source)
XLA Modules:
  0.0 22.9 jit_solution(16435177301959224084)
XLA Ops:
  0.6 21.5 %shard_map.86 = (f32[4,31,384]{2,1,0:T(8,128)S(1)}, f32[2,31,384]{2,1,0:T(8,128)S(1)}) custom-call(f32[1,31,4,384]{3,2,1,0:T(4,128)} %bitcast.4, f32[1,31,2,384]{3,2,1,0:T(2,128)} %bitcast.5, s32[31,384]{1,0:T(8,128)} %wet_hbm.1, s32[1,1,279]{2,1,0:T(1,128)} %source_hbm.1, s32[1,1,279]{2,1,0:T(1,128)} %dest_hbm.1, s32[1,1,279]{2,1,0:T(1,128)} %block_hbm.1, ...), custom_call_target="tpu_custom_call" | custom-call | tf_op jit(solution)/shard_map/pallas_call | solution.py:462
  22.1 0.8 %shard_map.87 = (f32[1,31,4,384]{3,2,1,0:T(4,128)}, f32[1,31,2,384]{3,2,1,0:T(2,128)}) custom-call(f32[4,31,384]{2,1,0:T(8,128)S(1)} %get-tuple-element.6.new, f32[2,31,384]{2,1,0:T(8,128)S(1)} %get-tuple-element.7.coupled), custom_call_target="tpu_custom_call" | custom-call | tf_op jit(solution)/shard_map/pallas_call | solution.py:495
